TPU v7x, 128 devices: a whole 4x4x4 slice. The times are simulated.
128 devices in a mesh: red: 4 (over z), ten: 32 (over y, x, core).
Axes of the slice: x: 4, y: 4, z: 4, core: 2. Of those that a mesh axis runs over, the one named last changes fastest.
Arguments:
- amps: bfloat16 [1024, 32768], P('red', 'ten'), may hold values from -6 to 6
- ladder_ints: bfloat16 [256, 48, 128, 128], P('ten', 'red'), may hold values from -0.09375 to 0.09375
- cycle_ints: bfloat16 [256, 48, 128, 128], P('ten', 'red'), may hold values from -0.09375 to 0.09375
- sym_sizes: int32 [8], replicated, may hold values from 1 to 48, 256 in all
- occ_energy: float32 [1024], P('red'), may hold values from -2 to -0.5
- vir_energy: float32 [32768], P('ten'), may hold values from 0.5 to 2.5
Outputs:
- update: float32 [1024, 32768], P('red', 'ten')
Inputs may be any that keep to these rules, and one draw needn't show every extreme that they name: sym_sizes sum to 256; the largest is exactly 48.
All inputs are finite; a program needn't handle non-finite values.
Results may differ from a plain program's by a relative error of at most 0.0029.
Values may be sent and summed in bfloat16 or wider, within the bound.
A program may use at most 320 MiB of HBM per device.

v0:
```python
import jax
import jax.numpy as jnp
from jax import lax
from jax.sharding import PartitionSpec as P

PB_DEV = 8
SLOTS = 48


def from_behind(value, axis, steps):
    count = lax.axis_size(axis)
    first, last = (max(0, -steps), min(count, count - steps))
    return lax.ppermute(value, axis, [(source, source + steps) for source in range(first, last)])


def widen(operand):
    ten_at = lax.axis_index("ten")
    reach_dev = (SLOTS + PB_DEV - 2) // PB_DEV
    pieces = []
    for distance in range(reach_dev, -reach_dev - 1, -1):
        if distance == 0:
            pieces.append(operand)
        else:
            pieces.append(from_behind(operand, "ten", distance))
    widened = jnp.concatenate(pieces, axis=1)
    return (widened, (ten_at - reach_dev) * PB_DEV)


def contract(widened, base, tiles, sym_sizes, slot_first):
    blocks_here = tiles.shape[0]
    share_slots = tiles.shape[1]
    width = tiles.shape[2]
    row_count = widened.shape[0]
    ten_at = lax.axis_index("ten")
    sym_ends = jnp.cumsum(sym_sizes)
    starts = sym_ends - sym_sizes
    slot_index = jnp.arange(share_slots * width, dtype=jnp.int32) // width + slot_first

    def one_block(local_block):
        block_at = ten_at * blocks_here + local_block
        member = (starts <= block_at) & (block_at < sym_ends)
        first_block = jnp.sum(jnp.where(member, starts, 0))
        block_count = jnp.sum(jnp.where(member, sym_sizes, 0))
        col_start = (first_block - base + slot_first) * width
        columns = lax.dynamic_slice_in_dim(widened, col_start, share_slots * width, 1)
        slot_mask = (slot_index < block_count).astype(jnp.bfloat16)
        tile_block = lax.dynamic_index_in_dim(tiles, local_block, 0, keepdims=False)
        return jnp.dot(
            columns * slot_mask[None, :],
            tile_block.reshape(share_slots * width, width),
            preferred_element_type=jnp.float32,
        )

    blocks = lax.map(one_block, jnp.arange(blocks_here, dtype=jnp.int32))
    return jnp.transpose(blocks, (1, 0, 2)).reshape(row_count, blocks_here * width)


def shards(amps, ladder_ints, cycle_ints, sym_sizes, occ_energy, vir_energy):
    denom = vir_energy[None, :] - occ_energy[:, None]
    ladder_full, cycle_full = (
        lax.all_gather(ladder_ints, "red", axis=1, tiled=True),
        lax.all_gather(cycle_ints, "red", axis=1, tiled=True),
    )
    widened, base = widen(amps)
    ladder = contract(widened, base, ladder_full, sym_sizes, 0)
    dressed = (amps.astype(jnp.float32) + ladder / denom).astype(jnp.bfloat16)
    widened, base = widen(dressed)
    cycle = contract(widened, base, cycle_full, sym_sizes, 0)
    return dressed.astype(jnp.float32) + cycle / denom


def solution(mesh):
    placed = (
        P("red", "ten"),
        P("ten", "red", None, None),
        P("ten", "red", None, None),
        P(),
        P("red"),
        P("ten"),
    )
    return jax.shard_map(
        shards, mesh=mesh, in_specs=placed, out_specs=P("red", "ten"), check_vma=False
    )
```

profile of v0, /device:TPU:6, one launch (start us, length us, event | category | flops | bytes accessed | tf_op | source)
XLA Modules:
  0.0 413.2 jit_solution(273308855188948571)
XLA Ops:
  8.0 3.8 collective-permute-start
  11.8 3.2 collective-permute-start.1
  15.0 4.3 %collective-permute-start.2 = (bf16[256,1024]{1,0:T(8,128)(2,1)}, bf16[256,1024]{1,0:T(8,128)(2,1)S(1)}, u32[]{:S(2)}, u32[]{:S(2)}) collective-permute-start(bf16[256,1024]{1,0:T(8,128)(2,1)} %param.10), channel_id=1, source_target_pairs={{0,4},{1,5},{2,6},{3,7},{4,8},{5,9},{6,10},{7,11},{8,12},{9,13},{1... | collective-permute-start | bytes 1572872 | tf_op jit(solution)/shard_map/ppermute | solution.py:13
  19.3 3.1 collective-permute-start.3
  22.4 3.1 collective-permute-start.4
  27.1 3.2 collective-permute-start.5
  31.2 4.4 %collective-permute-done.1 = bf16[256,1024]{1,0:T(8,128)(2,1)S(1)} collective-permute-done((bf16[256,1024]{1,0:T(8,128)(2,1)}, bf16[256,1024]{1,0:T(8,128)(2,1)S(1)}, u32[]{:S(2)}, u32[]{:S(2)}) %collective-permute-start.1) | collective-permute-done | bytes 524320 | tf_op jit(solution)/shard_map/ppermute | solution.py:13
  38.4 20.5 %collective-permute-done.2 = bf16[256,1024]{1,0:T(8,128)(2,1)S(1)} collective-permute-done((bf16[256,1024]{1,0:T(8,128)(2,1)}, bf16[256,1024]{1,0:T(8,128)(2,1)S(1)}, u32[]{:S(2)}, u32[]{:S(2)}) %collective-permute-start.2) | collective-permute-done | bytes 524320 | tf_op jit(solution)/shard_map/ppermute | solution.py:13
  61.8 6.1 %collective-permute-done.3 = bf16[256,1024]{1,0:T(8,128)(2,1)S(1)} collective-permute-done((bf16[256,1024]{1,0:T(8,128)(2,1)}, bf16[256,1024]{1,0:T(8,128)(2,1)S(1)}, u32[]{:S(2)}, u32[]{:S(2)}) %collective-permute-start.3) | collective-permute-done | bytes 524320 | tf_op jit(solution)/shard_map/ppermute | solution.py:13
  70.7 4.8 %collective-permute-done.4 = bf16[256,1024]{1,0:T(8,128)(2,1)S(1)} collective-permute-done((bf16[256,1024]{1,0:T(8,128)(2,1)}, bf16[256,1024]{1,0:T(8,128)(2,1)S(1)}, u32[]{:S(2)}, u32[]{:S(2)}) %collective-permute-start.4) | collective-permute-done | bytes 524320 | tf_op jit(solution)/shard_map/ppermute | solution.py:13
  84.7 3.1 collective-permute-done.7
  92.2 12.8 %collective-permute-done.9 = bf16[256,1024]{1,0:T(8,128)(2,1)S(1)} collective-permute-done((bf16[256,1024]{1,0:T(8,128)(2,1)S(1)}, bf16[256,1024]{1,0:T(8,128)(2,1)S(1)}, u32[]{:S(2)}, u32[]{:S(2)}) %collective-permute-start.9) | collective-permute-done | bytes 524320 | tf_op jit(solution)/shard_map/ppermute | solution.py:13
  105.9 3.6 collective-permute-done.10
  110.3 21.1 %collective-permute-done.11 = bf16[256,1024]{1,0:T(8,128)(2,1)S(1)} collective-permute-done((bf16[256,1024]{1,0:T(8,128)(2,1)S(1)}, bf16[256,1024]{1,0:T(8,128)(2,1)S(1)}, u32[]{:S(2)}, u32[]{:S(2)}) %collective-permute-start.11) | collective-permute-done | bytes 524320 | tf_op jit(solution)/shard_map/ppermute | solution.py:13
  132.4 74.2 %while.26 = (s32[]{:T(128)}, f32[8,256,128]{2,1,0:T(8,128)S(1)}, s32[8]{0:T(128)S(1)}, s32[]{:T(128)}, s32[8]{0:T(128)S(1)}, /*index=5*/s32[8]{0:T(128)S(1)}, s3...) while((s32[]{:T(128)}, f32[8,256,128]{2,1,0:T(8,128)S(1)}, ...), condition=%wide.region_4.5_spmd.clone, body=%wide.region_1.4_spmd.clone.sunk | while | flops 409006144 | bytes 8020857 | solution.py:54
  148.1 3.2 fusion.54
  175.9 3.0 fusion.54
  185.2 3.0 fusion.54
  194.4 3.0 fusion.54
  211.4 4.3 %collective-permute-start.14 = (bf16[256,1024]{1,0:T(8,128)(2,1)S(1)}, bf16[256,1024]{1,0:T(8,128)(2,1)S(1)}, u32[]{:S(2)}, u32[]{:S(2)}) collective-permute-start(bf16[256,1024]{1,0:T(8,128)(2,1)S(1)} %fusion.37), channel_id=1, source_target_pairs={{0,4},{1,5},{2,6},{3,7},{4,8},{5,9},{6,10},{7,11},{8,12},{9,13},{1... | collective-permute-start | bytes 1572872 | tf_op jit(solution)/shard_map/ppermute | solution.py:13
  215.7 3.1 collective-permute-start.15
  218.8 3.1 collective-permute-start.16
  221.9 3.0 collective-permute-done.12
  227.7 4.8 %collective-permute-done.13 = bf16[256,1024]{1,0:T(8,128)(2,1)S(1)} collective-permute-done((bf16[256,1024]{1,0:T(8,128)(2,1)S(1)}, bf16[256,1024]{1,0:T(8,128)(2,1)S(1)}, u32[]{:S(2)}, u32[]{:S(2)}) %collective-permute-start.13) | collective-permute-done | bytes 524320 | tf_op jit(solution)/shard_map/ppermute | solution.py:13
  235.2 20.1 %collective-permute-done.14 = bf16[256,1024]{1,0:T(8,128)(2,1)S(1)} collective-permute-done((bf16[256,1024]{1,0:T(8,128)(2,1)S(1)}, bf16[256,1024]{1,0:T(8,128)(2,1)S(1)}, u32[]{:S(2)}, u32[]{:S(2)}) %collective-permute-start.14) | collective-permute-done | bytes 524320 | tf_op jit(solution)/shard_map/ppermute | solution.py:13
  258.1 6.2 %collective-permute-done.15 = bf16[256,1024]{1,0:T(8,128)(2,1)S(1)} collective-permute-done((bf16[256,1024]{1,0:T(8,128)(2,1)S(1)}, bf16[256,1024]{1,0:T(8,128)(2,1)S(1)}, u32[]{:S(2)}, u32[]{:S(2)}) %collective-permute-start.15) | collective-permute-done | bytes 524320 | tf_op jit(solution)/shard_map/ppermute | solution.py:13
  267.1 4.6 %collective-permute-done.16 = bf16[256,1024]{1,0:T(8,128)(2,1)S(1)} collective-permute-done((bf16[256,1024]{1,0:T(8,128)(2,1)S(1)}, bf16[256,1024]{1,0:T(8,128)(2,1)S(1)}, u32[]{:S(2)}, u32[]{:S(2)}) %collective-permute-start.16) | collective-permute-done | bytes 524320 | tf_op jit(solution)/shard_map/ppermute | solution.py:13
  280.8 3.2 collective-permute-done.19
  288.6 12.7 %collective-permute-done.21 = bf16[256,1024]{1,0:T(8,128)(2,1)S(1)} collective-permute-done((bf16[256,1024]{1,0:T(8,128)(2,1)S(1)}, bf16[256,1024]{1,0:T(8,128)(2,1)S(1)}, u32[]{:S(2)}, u32[]{:S(2)}) %collective-permute-start.21) | collective-permute-done | bytes 524320 | tf_op jit(solution)/shard_map/ppermute | solution.py:13
  302.2 3.6 collective-permute-done.22
  306.6 21.1 %collective-permute-done.23 = bf16[256,1024]{1,0:T(8,128)(2,1)S(1)} collective-permute-done((bf16[256,1024]{1,0:T(8,128)(2,1)S(1)}, bf16[256,1024]{1,0:T(8,128)(2,1)S(1)}, u32[]{:S(2)}, u32[]{:S(2)}) %collective-permute-start.23) | collective-permute-done | bytes 524320 | tf_op jit(solution)/shard_map/ppermute | solution.py:13
  328.7 76.4 %while.27 = (s32[]{:T(128)}, f32[8,256,128]{2,1,0:T(8,128)S(1)}, s32[8]{0:T(128)S(1)}, s32[]{:T(128)}, s32[8]{0:T(128)S(1)}, /*index=5*/s32[8]{0:T(128)S(1)}, s3...) while((s32[]{:T(128)}, f32[8,256,128]{2,1,0:T(8,128)S(1)}, ...), condition=%wide.region_8.9_spmd.clone, body=%wide.region_5.8_spmd.clone.sunk | while | flops 409006144 | bytes 8020857 | solution.py:54
  (146 shorter events, 151.4 us)
Async XLA Ops:
  6.5 29.1 %copy-start = (bf16[256,1024]{1,0:T(8,128)(2,1)S(1)}, bf16[256,1024]{1,0:T(8,128)(2,1)}, u32[]{:S(2)}) copy-start(bf16[256,1024]{1,0:T(8,128)(2,1)} %param.10) | copy-start | bytes 1572868
  6.5 125.8 %all-gather.3.cloned.1.call-start = ((), (), s32[]{:S(2)}) async-start(), calls=%async_computation | async-start | bytes 15728640 | tf_op jit(solution)/shard_map/all_gather | solution.py:61
  7.3 321.4 %all-gather.5.cloned.1.call-start = ((), (), s32[]{:S(2)}) async-start(), calls=%async_computation.1 | async-start | bytes 15728640 | tf_op jit(solution)/shard_map/all_gather | solution.py:62
  8.0 19.1 %collective-permute-start = (bf16[256,1024]{1,0:T(8,128)(2,1)}, bf16[256,1024]{1,0:T(8,128)(2,1)S(1)}, u32[]{:S(2)}, u32[]{:S(2)}) collective-permute-start(bf16[256,1024]{1,0:T(8,128)(2,1)} %param.10), channel_id=1, source_target_pairs={{0,6},{1,7},{2,8},{3,9},{4,10},{5,11},{6,12},{7,13},{8,14},{9,15},... | collective-permute-start | bytes 1572872 | tf_op jit(solution)/shard_map/ppermute | solution.py:13
  11.8 23.9 %collective-permute-start.1 = (bf16[256,1024]{1,0:T(8,128)(2,1)}, bf16[256,1024]{1,0:T(8,128)(2,1)S(1)}, u32[]{:S(2)}, u32[]{:S(2)}) collective-permute-start(bf16[256,1024]{1,0:T(8,128)(2,1)} %param.10), channel_id=1, source_target_pairs={{0,5},{1,6},{2,7},{3,8},{4,9},{5,10},{6,11},{7,12},{8,13},{9,14},{... | collective-permute-start | bytes 1572872 | tf_op jit(solution)/shard_map/ppermute | solution.py:13
  15.0 44.0 %collective-permute-start.2 = (bf16[256,1024]{1,0:T(8,128)(2,1)}, bf16[256,1024]{1,0:T(8,128)(2,1)S(1)}, u32[]{:S(2)}, u32[]{:S(2)}) collective-permute-start(bf16[256,1024]{1,0:T(8,128)(2,1)} %param.10), channel_id=1, source_target_pairs={{0,4},{1,5},{2,6},{3,7},{4,8},{5,9},{6,10},{7,11},{8,12},{9,13},{1... | collective-permute-start | bytes 1572872 | tf_op jit(solution)/shard_map/ppermute | solution.py:13
  19.3 48.6 %collective-permute-start.3 = (bf16[256,1024]{1,0:T(8,128)(2,1)}, bf16[256,1024]{1,0:T(8,128)(2,1)S(1)}, u32[]{:S(2)}, u32[]{:S(2)}) collective-permute-start(bf16[256,1024]{1,0:T(8,128)(2,1)} %param.10), channel_id=1, source_target_pairs={{0,3},{1,4},{2,5},{3,6},{4,7},{5,8},{6,9},{7,10},{8,11},{9,12},{10... | collective-permute-start | bytes 1572872 | tf_op jit(solution)/shard_map/ppermute | solution.py:13
  22.4 53.1 %collective-permute-start.4 = (bf16[256,1024]{1,0:T(8,128)(2,1)}, bf16[256,1024]{1,0:T(8,128)(2,1)S(1)}, u32[]{:S(2)}, u32[]{:S(2)}) collective-permute-start(bf16[256,1024]{1,0:T(8,128)(2,1)} %param.10), channel_id=1, source_target_pairs={{0,2},{1,3},{2,4},{3,5},{4,6},{5,7},{6,8},{7,9},{8,10},{9,11},{10,... | collective-permute-start | bytes 1572872 | tf_op jit(solution)/shard_map/ppermute | solution.py:13
  27.1 51.2 %collective-permute-start.5 = (bf16[256,1024]{1,0:T(8,128)(2,1)}, bf16[256,1024]{1,0:T(8,128)(2,1)S(1)}, u32[]{:S(2)}, u32[]{:S(2)}) collective-permute-start(bf16[256,1024]{1,0:T(8,128)(2,1)} %param.10), channel_id=1, source_target_pairs={{0,1},{1,2},{2,3},{3,4},{4,5},{5,6},{6,7},{7,8},{8,9},{9,10},{10,1... | collective-permute-start | bytes 1572872 | tf_op jit(solution)/shard_map/ppermute | solution.py:13
  31.2 101.2 %copy-start.1 = (s32[8]{0:T(128)S(1)}, s32[8]{0:T(128)}, u32[]{:S(2)}) copy-start(s32[8]{0:T(128)} %param.13) | copy-start | bytes 100
  35.6 46.3 %collective-permute-start.6 = (bf16[256,1024]{1,0:T(8,128)(2,1)S(1)}, bf16[256,1024]{1,0:T(8,128)(2,1)S(1)}, u32[]{:S(2)}, u32[]{:S(2)}) collective-permute-start(bf16[256,1024]{1,0:T(8,128)(2,1)S(1)} %copy-done), channel_id=1, source_target_pairs={{1,0},{2,1},{3,2},{4,3},{5,4},{6,5},{7,6},{8,7},{9,8},{10,9},{11,1... | collective-permute-start | bytes 1572872 | tf_op jit(solution)/shard_map/ppermute | solution.py:13
  59.0 28.9 %collective-permute-start.7 = (bf16[256,1024]{1,0:T(8,128)(2,1)S(1)}, bf16[256,1024]{1,0:T(8,128)(2,1)S(1)}, u32[]{:S(2)}, u32[]{:S(2)}) collective-permute-start(bf16[256,1024]{1,0:T(8,128)(2,1)S(1)} %copy-done), channel_id=1, source_target_pairs={{2,0},{3,1},{4,2},{5,3},{6,4},{7,5},{8,6},{9,7},{10,8},{11,9},{12,... | collective-permute-start | bytes 1572872 | tf_op jit(solution)/shard_map/ppermute | solution.py:13
  67.9 23.5 %collective-permute-start.8 = (bf16[256,1024]{1,0:T(8,128)(2,1)S(1)}, bf16[256,1024]{1,0:T(8,128)(2,1)S(1)}, u32[]{:S(2)}, u32[]{:S(2)}) collective-permute-start(bf16[256,1024]{1,0:T(8,128)(2,1)S(1)} %copy-done), channel_id=1, source_target_pairs={{3,0},{4,1},{5,2},{6,3},{7,4},{8,5},{9,6},{10,7},{11,8},{12,9},{13... | collective-permute-start | bytes 1572872 | tf_op jit(solution)/shard_map/ppermute | solution.py:13
  75.5 29.5 %collective-permute-start.9 = (bf16[256,1024]{1,0:T(8,128)(2,1)S(1)}, bf16[256,1024]{1,0:T(8,128)(2,1)S(1)}, u32[]{:S(2)}, u32[]{:S(2)}) collective-permute-start(bf16[256,1024]{1,0:T(8,128)(2,1)S(1)} %copy-done), channel_id=1, source_target_pairs={{4,0},{5,1},{6,2},{7,3},{8,4},{9,5},{10,6},{11,7},{12,8},{13,9},{1... | collective-permute-start | bytes 1572872 | tf_op jit(solution)/shard_map/ppermute | solution.py:13
  78.3 31.2 %collective-permute-start.10 = (bf16[256,1024]{1,0:T(8,128)(2,1)S(1)}, bf16[256,1024]{1,0:T(8,128)(2,1)S(1)}, u32[]{:S(2)}, u32[]{:S(2)}) collective-permute-start(bf16[256,1024]{1,0:T(8,128)(2,1)S(1)} %copy-done), channel_id=1, source_target_pairs={{5,0},{6,1},{7,2},{8,3},{9,4},{10,5},{11,6},{12,7},{13,8},{14,9},{... | collective-permute-start | bytes 1572872 | tf_op jit(solution)/shard_map/ppermute | solution.py:13
  82.0 49.5 %collective-permute-start.11 = (bf16[256,1024]{1,0:T(8,128)(2,1)S(1)}, bf16[256,1024]{1,0:T(8,128)(2,1)S(1)}, u32[]{:S(2)}, u32[]{:S(2)}) collective-permute-start(bf16[256,1024]{1,0:T(8,128)(2,1)S(1)} %copy-done), channel_id=1, source_target_pairs={{6,0},{7,1},{8,2},{9,3},{10,4},{11,5},{12,6},{13,7},{14,8},{15,9},... | collective-permute-start | bytes 1572872 | tf_op jit(solution)/shard_map/ppermute | solution.py:13
  132.4 74.2 %copy-start.2 = (f32[1024]{0:T(1024)S(1)}, f32[1024]{0:T(1024)}, u32[]{:S(2)}) copy-start(f32[1024]{0:T(1024)} %param.15) | copy-start | bytes 12292
  132.4 74.2 %copy-start.3 = (f32[256]{0:T(256)S(1)}, f32[256]{0:T(256)}, u32[]{:S(2)}) copy-start(f32[256]{0:T(256)} %param.14) | copy-start | bytes 3076
  206.9 18.0 %collective-permute-start.12 = (bf16[256,1024]{1,0:T(8,128)(2,1)S(1)}, bf16[256,1024]{1,0:T(8,128)(2,1)S(1)}, u32[]{:S(2)}, u32[]{:S(2)}) collective-permute-start(bf16[256,1024]{1,0:T(8,128)(2,1)S(1)} %fusion.37), channel_id=1, source_target_pairs={{0,6},{1,7},{2,8},{3,9},{4,10},{5,11},{6,12},{7,13},{8,14},{9,15},... | collective-permute-start | bytes 1572872 | tf_op jit(solution)/shard_map/ppermute | solution.py:13
  208.9 23.6 %collective-permute-start.13 = (bf16[256,1024]{1,0:T(8,128)(2,1)S(1)}, bf16[256,1024]{1,0:T(8,128)(2,1)S(1)}, u32[]{:S(2)}, u32[]{:S(2)}) collective-permute-start(bf16[256,1024]{1,0:T(8,128)(2,1)S(1)} %fusion.37), channel_id=1, source_target_pairs={{0,5},{1,6},{2,7},{3,8},{4,9},{5,10},{6,11},{7,12},{8,13},{9,14},{... | collective-permute-start | bytes 1572872 | tf_op jit(solution)/shard_map/ppermute | solution.py:13
  211.4 44.0 %collective-permute-start.14 = (bf16[256,1024]{1,0:T(8,128)(2,1)S(1)}, bf16[256,1024]{1,0:T(8,128)(2,1)S(1)}, u32[]{:S(2)}, u32[]{:S(2)}) collective-permute-start(bf16[256,1024]{1,0:T(8,128)(2,1)S(1)} %fusion.37), channel_id=1, source_target_pairs={{0,4},{1,5},{2,6},{3,7},{4,8},{5,9},{6,10},{7,11},{8,12},{9,13},{1... | collective-permute-start | bytes 1572872 | tf_op jit(solution)/shard_map/ppermute | solution.py:13
  215.7 48.6 %collective-permute-start.15 = (bf16[256,1024]{1,0:T(8,128)(2,1)S(1)}, bf16[256,1024]{1,0:T(8,128)(2,1)S(1)}, u32[]{:S(2)}, u32[]{:S(2)}) collective-permute-start(bf16[256,1024]{1,0:T(8,128)(2,1)S(1)} %fusion.37), channel_id=1, source_target_pairs={{0,3},{1,4},{2,5},{3,6},{4,7},{5,8},{6,9},{7,10},{8,11},{9,12},{10... | collective-permute-start | bytes 1572872 | tf_op jit(solution)/shard_map/ppermute | solution.py:13
  218.8 52.9 %collective-permute-start.16 = (bf16[256,1024]{1,0:T(8,128)(2,1)S(1)}, bf16[256,1024]{1,0:T(8,128)(2,1)S(1)}, u32[]{:S(2)}, u32[]{:S(2)}) collective-permute-start(bf16[256,1024]{1,0:T(8,128)(2,1)S(1)} %fusion.37), channel_id=1, source_target_pairs={{0,2},{1,3},{2,4},{3,5},{4,6},{5,7},{6,8},{7,9},{8,10},{9,11},{10,... | collective-permute-start | bytes 1572872 | tf_op jit(solution)/shard_map/ppermute | solution.py:13
  224.9 49.5 %collective-permute-start.17 = (bf16[256,1024]{1,0:T(8,128)(2,1)S(1)}, bf16[256,1024]{1,0:T(8,128)(2,1)S(1)}, u32[]{:S(2)}, u32[]{:S(2)}) collective-permute-start(bf16[256,1024]{1,0:T(8,128)(2,1)S(1)} %fusion.37), channel_id=1, source_target_pairs={{0,1},{1,2},{2,3},{3,4},{4,5},{5,6},{6,7},{7,8},{8,9},{9,10},{10,1... | collective-permute-start | bytes 1572872 | tf_op jit(solution)/shard_map/ppermute | solution.py:13
  232.5 45.6 %collective-permute-start.18 = (bf16[256,1024]{1,0:T(8,128)(2,1)S(1)}, bf16[256,1024]{1,0:T(8,128)(2,1)S(1)}, u32[]{:S(2)}, u32[]{:S(2)}) collective-permute-start(bf16[256,1024]{1,0:T(8,128)(2,1)S(1)} %fusion.37), channel_id=1, source_target_pairs={{1,0},{2,1},{3,2},{4,3},{5,4},{6,5},{7,6},{8,7},{9,8},{10,9},{11,1... | collective-permute-start | bytes 1572872 | tf_op jit(solution)/shard_map/ppermute | solution.py:13
  255.4 28.7 %collective-permute-start.19 = (bf16[256,1024]{1,0:T(8,128)(2,1)S(1)}, bf16[256,1024]{1,0:T(8,128)(2,1)S(1)}, u32[]{:S(2)}, u32[]{:S(2)}) collective-permute-start(bf16[256,1024]{1,0:T(8,128)(2,1)S(1)} %fusion.37), channel_id=1, source_target_pairs={{2,0},{3,1},{4,2},{5,3},{6,4},{7,5},{8,6},{9,7},{10,8},{11,9},{12,... | collective-permute-start | bytes 1572872 | tf_op jit(solution)/shard_map/ppermute | solution.py:13
  264.3 23.4 %collective-permute-start.20 = (bf16[256,1024]{1,0:T(8,128)(2,1)S(1)}, bf16[256,1024]{1,0:T(8,128)(2,1)S(1)}, u32[]{:S(2)}, u32[]{:S(2)}) collective-permute-start(bf16[256,1024]{1,0:T(8,128)(2,1)S(1)} %fusion.37), channel_id=1, source_target_pairs={{3,0},{4,1},{5,2},{6,3},{7,4},{8,5},{9,6},{10,7},{11,8},{12,9},{13... | collective-permute-start | bytes 1572872 | tf_op jit(solution)/shard_map/ppermute | solution.py:13
  271.7 29.6 %collective-permute-start.21 = (bf16[256,1024]{1,0:T(8,128)(2,1)S(1)}, bf16[256,1024]{1,0:T(8,128)(2,1)S(1)}, u32[]{:S(2)}, u32[]{:S(2)}) collective-permute-start(bf16[256,1024]{1,0:T(8,128)(2,1)S(1)} %fusion.37), channel_id=1, source_target_pairs={{4,0},{5,1},{6,2},{7,3},{8,4},{9,5},{10,6},{11,7},{12,8},{13,9},{1... | collective-permute-start | bytes 1572872 | tf_op jit(solution)/shard_map/ppermute | solution.py:13
  274.4 31.4 %collective-permute-start.22 = (bf16[256,1024]{1,0:T(8,128)(2,1)S(1)}, bf16[256,1024]{1,0:T(8,128)(2,1)S(1)}, u32[]{:S(2)}, u32[]{:S(2)}) collective-permute-start(bf16[256,1024]{1,0:T(8,128)(2,1)S(1)} %fusion.37), channel_id=1, source_target_pairs={{5,0},{6,1},{7,2},{8,3},{9,4},{10,5},{11,6},{12,7},{13,8},{14,9},{... | collective-permute-start | bytes 1572872 | tf_op jit(solution)/shard_map/ppermute | solution.py:13
  278.0 49.7 %collective-permute-start.23 = (bf16[256,1024]{1,0:T(8,128)(2,1)S(1)}, bf16[256,1024]{1,0:T(8,128)(2,1)S(1)}, u32[]{:S(2)}, u32[]{:S(2)}) collective-permute-start(bf16[256,1024]{1,0:T(8,128)(2,1)S(1)} %fusion.37), channel_id=1, source_target_pairs={{6,0},{7,1},{8,2},{9,3},{10,4},{11,5},{12,6},{13,7},{14,8},{15,9},... | collective-permute-start | bytes 1572872 | tf_op jit(solution)/shard_map/ppermute | solution.py:13
Sparse Core Ops, SparseCore 0:
  9.0 120.9 all-gather.2
  131.7 119.6 all-gather.4
where the time goes:
time: 416 us; the launch traced here: 413 us
  waiting for transfers between devices  163 us (39%)
  starting transfers between devices  60.5 us (15%)
  local copies, waits for them, and re-layouts  56.4 us (14%)
  loops' own time  48.8 us (12%)
  matrix products  46.9 us (11%)
  other arithmetic  24 us (6%)
  between operations  13.7 us (3%)
    ppermute x24, waiting for transfers between devices, from_behind(): lax.ppermute(value, axis, [(source, source + steps) for source in range(f...  161 us
    ppermute x24, starting transfers between devices, from_behind(): lax.ppermute(value, axis, [(source, source + steps) for source in range(f...  60.5 us
    another operation x2, loops' own time, contract(): blocks = lax.map(one_block, jnp.arange(blocks_here, dtype=jnp.int32))  48.8 us
    dot_general x16, matrix products, one_block(): jnp.dot(columns * slot_mask[None, :], tile_block.reshape(share_slots * wi...  46.9 us
    dynamic_slice x16, local copies, waits for them, and re-layouts, one_block(): tile_block = lax.dynamic_index_in_dim(tiles, local_block, 0, keepdims=False)  24.4 us
    unnamed x32, local copies, waits for them, and re-layouts  20.7 us
    reduce_sum x16, other arithmetic, one_block(): block_count = jnp.sum(jnp.where(member, sym_sizes, 0))  10.9 us
    convert_element_type x16, other arithmetic, one_block(): slot_mask = (slot_index < block_count).astype(jnp.bfloat16)  10.1 us
  transfers between devices with their start and end apart: 26, of which 19 were waited for; matrix products, arithmetic and copies ran while one was open for 18% of the time, Pallas kernels for 0%

commit v1 on v0

v1 whole, which is shorter than its diff:
```python
import functools

import jax
import jax.numpy as jnp
from jax import lax
from jax.experimental import pallas as pl
from jax.experimental.pallas import tpu as pltpu
from jax.sharding import PartitionSpec as P

MESH = pl.DeviceIdType.MESH
NZ = 4
NX = 4
BS = 128
SLOTS = 12
DEVB = 8
CHIPB = 2 * DEVB
DW = DEVB * BS
KW = SLOTS * BS
INNER = 14
WIN = 7 * CHIPB
HERE = 3 * CHIPB
CHUNKS = 2
ROWS = 128
M = ROWS // CHUNKS


def remote(src, dst, send, recv, device):
    return pltpu.make_async_remote_copy(
        src_ref=src,
        dst_ref=dst,
        send_sem=send,
        recv_sem=recv,
        device_id=device,
        device_id_type=MESH,
    )


def kernel(inner, sizes, amps, ints0, ints1, occ, vir, out, *scratch):
    scratch = list(scratch)

    def take(count):
        taken = scratch[:count]
        del scratch[:count]
        return taken

    win = [take(CHUNKS) for _ in range(2)]
    gathered = [take(CHUNKS) for _ in range(2)]
    packed = [take(CHUNKS) for _ in range(2)]
    packed_in = [take(CHUNKS) for _ in range(2)] if inner else None
    ints = take(2)
    part = take(CHUNKS)
    part_send = [take(CHUNKS) for _ in range(2)]
    part_recv = [take(CHUNKS) for _ in range(2)]
    (virs, stage, other_amps) = take(3)
    (x_s, x_r, y_s, y_r, z_s, z_r, zi_s, zi_r, p_s, p_r) = take(10)
    (w_s, w_r, w_l, a_s, a_r, v_s, v_r, o_s, o_r, o_l) = take(10)

    r = lax.axis_index("red")
    t = lax.axis_index("ten")
    h = lax.rem(t, 2)
    c = t // 2
    x = lax.rem(c, NX)
    y = c // NX

    def at(z, yy, xx, hh):
        return (z, (yy * NX + xx) * 2 + hh)

    sibling = at(r, y, x, 1 - h)

    def x_peer(d):
        return at(r, y, lax.rem(x + d, NX), h)

    def y_peer(d):
        return at(r, lax.rem(y + d + 4, 4), x, h)

    def z_to(d):
        return lax.rem(r + d, NZ)

    def z_peer(d):
        return at(z_to(d), y, x, h)

    peers = [sibling] + [x_peer(d) for d in (1, 2, 3)] + [y_peer(d) for d in (1, -1)]
    peers += [z_peer(d) for d in (1, 2, 3)]

    def group(block):
        start = jnp.int32(0)
        first, count = jnp.int32(0), jnp.int32(0)
        for g in range(8):
            size = sizes[g]
            inside = (start <= block) & (block < start + size)
            first = first + jnp.where(inside, start, 0)
            count = count + jnp.where(inside, size, 0)
            start = start + size
        return first, count

    head, head_n = group(c * CHIPB)
    tail, _ = group(c * CHIPB + CHIPB - 1)
    inner_at = jnp.minimum(head + head_n, (c + 1) * CHIPB)
    window_at = (c - 3) * CHIPB

    row0 = h * ROWS

    def sibling_amps(k):
        return remote(
            other_amps.at[k],
            win[0][k].at[pl.ds(HERE + h * DEVB, DEVB)],
            a_s.at[k],
            a_r.at[k],
            sibling,
        )

    def local_ints(p):
        return pltpu.make_async_copy(
            (ints0, ints1)[p], ints[p].at[pl.ds(h * DEVB, DEVB)], w_l.at[p]
        )

    def sibling_ints(p):
        return remote(
            (ints0, ints1)[p],
            ints[p].at[pl.ds(h * DEVB, DEVB)],
            w_s.at[p],
            w_r.at[p],
            sibling,
        )

    def sibling_vir():
        return remote(vir, virs.at[pl.ds(h * DEVB, DEVB)], v_s, v_r, sibling)

    def x_send(p, k, d):
        there = lax.rem(x + d, NX)
        return remote(
            win[p][k].at[pl.ds(HERE, CHIPB)],
            win[p][k].at[pl.ds((x - there + 3) * CHIPB, CHIPB)],
            x_s.at[p, k, d - 1],
            x_r.at[p, k, d - 1],
            x_peer(d),
        )

    def y_send(p, k, o):
        up = o > 0
        to = o - 4 if up else o + 4
        index = o + 3 if o < 0 else o + 2
        return remote(
            win[p][k].at[pl.ds((o + 3) * CHIPB, CHIPB)],
            win[p][k].at[pl.ds((to + 3) * CHIPB, CHIPB)],
            y_s.at[p, k, index],
            y_r.at[p, k, index],
            y_peer(1 if up else -1),
        )

    def y_each(p, k, act):
        for o in (-3, -2, -1, 1, 2, 3):
            has = (x + o <= 3) if o > 0 else (x + o >= 0)

            @pl.when(has)
            def _():
                act(y_send(p, k, o))

    def z_send(p, k, d):
        return remote(
            packed[p][k].at[d - 1],
            gathered[p][k].at[pl.ds(0, 2 * SLOTS), pl.ds(pl.multiple_of(r * M, M), M)],
            z_s.at[p, k, d - 1],
            z_r.at[p, k, d - 1],
            z_peer(d),
        )

    def zi_send(p, k, d):
        return remote(
            packed_in[p][k],
            gathered[p][k].at[
                pl.ds(2 * SLOTS, INNER), pl.ds(pl.multiple_of(r * M, M), M)
            ],
            zi_s.at[p, k, d - 1],
            zi_r.at[p, k, d - 1],
            z_peer(d),
        )

    def p_send(p, k, d):
        return remote(
            part_send[p][k].at[z_to(d)],
            part_recv[p][k].at[d - 1],
            p_s.at[p, k, d - 1],
            p_r.at[p, k, d - 1],
            z_peer(d),
        )

    def local_out(k):
        return pltpu.make_async_copy(
            stage.at[k, 0], out.at[pl.ds(row0 + k * M, M), :], o_l.at[k]
        )

    def sibling_out(k):
        return remote(
            stage.at[k, 1],
            out.at[pl.ds(row0 + k * M, M), :],
            o_s.at[k],
            o_r.at[k],
            sibling,
        )

    barrier = pltpu.get_barrier_semaphore()
    for peer in peers:
        pl.semaphore_signal(barrier, inc=1, device_id=peer, device_id_type=MESH)
    for p in range(2):
        local_ints(p).start()
    for k in range(CHUNKS):
        mine = pl.ds(pl.multiple_of(row0 + k * M, M), M)
        theirs = pl.ds(pl.multiple_of((1 - h) * ROWS + k * M, M), M)
        for b in range(DEVB):
            columns = slice(b * BS, (b + 1) * BS)
            win[0][k][HERE + h * DEVB + b] = amps[mine, columns]
            other_amps[k, b] = amps[theirs, columns]
    pl.semaphore_wait(barrier, len(peers))

    for k in range(CHUNKS):
        sibling_amps(k).start()
    sibling_vir().start()
    for p in range(2):
        sibling_ints(p).start()

    def spread_row(p, k):
        if p == 0:
            sibling_amps(k).wait_recv()
        for d in (1, 3, 2):
            x_send(p, k, d).start()

    def spread_rows(p, k):
        for d in (1, 2, 3):
            x_send(p, k, d).wait_recv()
        y_each(p, k, lambda copy: copy.start())

    def exchange(p, k):
        y_each(p, k, lambda copy: copy.wait_recv())
        source = win[p][k]

        def piece(first, plane):
            start = jnp.clip(first - window_at, 0, WIN - NZ * SLOTS)
            return source[pl.ds(start + plane * SLOTS, SLOTS)]

        for d in (1, 3, 2):
            packed[p][k][d - 1, 0:SLOTS] = piece(head, z_to(d))
            packed[p][k][d - 1, SLOTS : 2 * SLOTS] = piece(tail, z_to(d))
            z_send(p, k, d).start()
        rows = pl.ds(pl.multiple_of(r * M, M), M)
        if inner:
            between = source[pl.ds(jnp.clip(inner_at - window_at, 0, WIN - INNER), INNER)]
            packed_in[p][k][...] = between
            for d in (1, 2, 3):

                @pl.when(z_to(d) < 2)
                def _():
                    zi_send(p, k, d).start()

            gathered[p][k][2 * SLOTS : 2 * SLOTS + INNER, rows] = between
        gathered[p][k][0:SLOTS, rows] = piece(head, r)
        gathered[p][k][SLOTS : 2 * SLOTS, rows] = piece(tail, r)

    def multiply(p, k):
        for d in (1, 2, 3):
            z_send(p, k, d).wait_recv()
        if inner:

            @pl.when(r < 2)
            def _():
                for d in (1, 2, 3):
                    zi_send(p, k, d).wait_recv()

        @pl.loop(0, CHIPB)
        def _(q):
            first, count = group(c * CHIPB + q)
            base = jnp.where(first == head, 0, SLOTS)
            if inner:
                between = (first != head) & (first != tail)
                some = count > r * SLOTS
                place = 2 * SLOTS + first + r * SLOTS - inner_at
                base = jnp.where(between, jnp.where(some, place, 0), base)
                base = jnp.clip(base, 0, 2 * SLOTS + INNER - 1)
            tiles = gathered[p][k][pl.ds(base, SLOTS)]
            rows = jnp.concatenate([tiles[i] for i in range(SLOTS)], axis=1)
            product = jnp.dot(rows, ints[p][q], preferred_element_type=jnp.float32)
            product = product.reshape(NZ, M, BS)
            part[k][:, q] = product
            part_send[p][k][:, q] = product.astype(jnp.bfloat16)

        for d in (1, 3, 2):
            p_send(p, k, d).start()

    def finish(p, k):
        for d in (1, 2, 3):
            p_send(p, k, d).wait_recv()

        own = pl.ds(pl.multiple_of(row0 + k * M, M), M)

        @pl.loop(0, DEVB)
        def _(b):
            for side in range(2):
                q = (h if side == 0 else 1 - h) * DEVB + b
                total = part[k][r, q]
                for d in range(3):
                    total += part_recv[p][k][d, q].astype(jnp.float32)
                denom = virs[q] - occ[own, :]
                value = win[p][k][HERE + q].astype(jnp.float32) + total / denom
                if p == 0:
                    win[1][k][HERE + q] = value.astype(jnp.bfloat16)
                else:
                    stage[k, side, :, pl.ds(pl.multiple_of(b * BS, BS), BS)] = value

        if p == 1:
            sibling_out(k).start()
            local_out(k).start()

    def mask(p):
        local_ints(p).wait()
        sibling_ints(p).wait_recv()
        slot = lax.broadcasted_iota(jnp.int32, (KW, BS), 0)

        @pl.loop(0, CHIPB)
        def _(q):
            _, count = group(c * CHIPB + q)
            limit = (count - r * SLOTS) * BS
            tile = ints[p][q]
            ints[p][q] = jnp.where(slot < limit, tile, jnp.zeros_like(tile))

    for b in range(DEVB):
        virs[h * DEVB + b] = vir[b]
    if inner:
        for p in range(2):
            for k in range(CHUNKS):
                for b in range(2 * SLOTS + INNER, 3 * SLOTS + INNER - 1):
                    gathered[p][k][b] = jnp.zeros((NZ * M, BS), jnp.bfloat16)

    for k in range(CHUNKS):
        spread_row(0, k)
    for k in range(CHUNKS):
        spread_rows(0, k)
    for p in range(2):
        for k in range(CHUNKS):
            exchange(p, k)
        if p == 0:
            mask(0)
            mask(1)
            sibling_vir().wait_recv()
        for k in range(CHUNKS):
            multiply(p, k)
        for k in range(CHUNKS):
            finish(p, k)
            if p == 0:
                spread_row(1, k)
        if p == 0:
            for k in range(CHUNKS):
                spread_rows(1, k)

    for p in range(2):
        sibling_ints(p).wait_send()
        for k in range(CHUNKS):
            for d in (1, 2, 3):
                x_send(p, k, d).wait_send()
                z_send(p, k, d).wait_send()
                p_send(p, k, d).wait_send()
                if inner:

                    @pl.when(z_to(d) < 2)
                    def _():
                        zi_send(p, k, d).wait_send()

            y_each(p, k, lambda copy: copy.wait_send())
    sibling_vir().wait_send()
    for k in range(CHUNKS):
        sibling_amps(k).wait_send()
        local_out(k).wait()
        sibling_out(k).wait()


def call(inner, number, operands):
    bf16, f32 = jnp.bfloat16, jnp.float32
    width = 2 * SLOTS + (INNER + SLOTS - 1 if inner else 0)
    vmem = pltpu.VMEM
    dma = pltpu.SemaphoreType.DMA
    each = []
    each += [vmem((WIN, M, BS), bf16)] * (2 * CHUNKS)
    each += [vmem((width, NZ * M, BS), bf16)] * (2 * CHUNKS)
    each += [vmem((3, 2 * SLOTS, M, BS), bf16)] * (2 * CHUNKS)
    if inner:
        each += [vmem((INNER, M, BS), bf16)] * (2 * CHUNKS)
    each += [vmem((CHIPB, KW, BS), bf16)] * 2
    each += [vmem((NZ, CHIPB, M, BS), f32)] * CHUNKS
    each += [vmem((NZ, CHIPB, M, BS), bf16)] * (2 * CHUNKS)
    each += [vmem((3, CHIPB, M, BS), bf16)] * (2 * CHUNKS)
    each += [vmem((CHIPB, 1, BS), f32), vmem((CHUNKS, 2, M, DW), f32)]
    each += [vmem((CHUNKS, DEVB, M, BS), bf16)]
    three, six = (2, CHUNKS, 3), (2, CHUNKS, 6)
    each += [dma(s) for s in (three, three, six, six, three, three, three, three, three, three)]
    each += [dma((2,))] * 3 + [dma((CHUNKS,))] * 2 + [dma(())] * 2 + [dma((CHUNKS,))] * 3
    hbm = pl.BlockSpec(memory_space=pl.ANY)
    return pl.pallas_call(
        functools.partial(kernel, inner),
        name="ladders",
        out_shape=jax.ShapeDtypeStruct((2 * ROWS, DW), f32),
        in_specs=[
            pl.BlockSpec(memory_space=pltpu.SMEM),
            pl.BlockSpec(memory_space=pltpu.VMEM),
            hbm,
            hbm,
            pl.BlockSpec(memory_space=pltpu.VMEM),
            pl.BlockSpec(memory_space=pltpu.VMEM),
        ],
        out_specs=hbm,
        scratch_shapes=each,
        compiler_params=pltpu.CompilerParams(
            collective_id=number, has_side_effects=True, vmem_limit_bytes=60 << 20
        ),
    )(*operands)


def shards(amps, ladder_ints, cycle_ints, sym_sizes, occ_energy, vir_energy):
    operands = (
        sym_sizes,
        amps,
        ladder_ints.reshape(DEVB, KW, BS),
        cycle_ints.reshape(DEVB, KW, BS),
        occ_energy[:, None],
        vir_energy.reshape(DEVB, 1, BS),
    )
    return call(True, 1, operands)


def solution(mesh):
    placed = (
        P("red", "ten"),
        P("ten", "red", None, None),
        P("ten", "red", None, None),
        P(),
        P("red"),
        P("ten"),
    )
    return jax.shard_map(
        shards, mesh=mesh, in_specs=placed, out_specs=P("red", "ten"), check_vma=False
    )
```

time: 416 us -> 225 us (0.54)
  the two profiles are of different devices: /device:TPU:6 before, /device:TPU:65 now
where the time goes in v1:
time: 225 us
  Pallas kernels  221 us (98%)
  local copies, waits for them, and re-layouts  3.78 us (2%)
    pallas_call x1, Pallas kernels, call(): pl.pallas_call(functools.partial(kernel, inner), name='ladders', out_shap...  221 us

profile of v1, /device:TPU:65, one launch (start us, length us, event | category | flops | bytes accessed | tf_op | source)
XLA Modules:
  0.0 224.9 jit_solution(8184431603024989296)
XLA Ops:
  0.0 1.5 copy.7.occ
  1.5 221.1 %ladders.1 = f32[256,1024]{1,0:T(8,128)} custom-call(s32[8]{0:T(128)} %sizes.1, bf16[256,1024]{1,0:T(8,128)(2,1)} %amps.1, bf16[8,1536,128]{2,1,0:T(8,128)(2,1)} %bitcast.4, bf16[8,1536,128]{2,1,0:T(8,128)(2,1)} %bitcast.5, f32[256,1]{1,0:T(8,128)} %copy.7.occ, f32[8,1,128]{2,1,0:T(1,128)} %bitcast.6), custom_call_target="tpu_custom_call" | custom-call | tf_op jit(solution)/shard_map/ladders/pallas_call | solution.py:396
  222.6 2.3 %copy.9 = f32[256,1024]{1,0:T(8,128)} copy(f32[256,1024]{1,0:T(8,128)} %ladders.1) | data formatting | bytes 2097152

commit v2 on v1

--- a/solution.py
+++ b/solution.py
@@ -19,7 +19,14 @@
 INNER = 14
 WIN = 7 * CHIPB
 HERE = 3 * CHIPB
-CHUNKS = 2
+CHUNKS = 8
+ORDER = tuple(
+    (tick - k // 2, k)
+    for tick in range(10 + CHUNKS // 2 - 1)
+    for k in reversed(range(CHUNKS))
+    if 0 < tick - k // 2 < 10
+)
+ORDER = tuple((0, k) for k in range(CHUNKS)) + ORDER
 ROWS = 128
 M = ROWS // CHUNKS
 
@@ -215,9 +222,6 @@
 
     for k in range(CHUNKS):
         sibling_amps(k).start()
-    sibling_vir().start()
-    for p in range(2):
-        sibling_ints(p).start()
 
     def spread_row(p, k):
         if p == 0:
@@ -330,26 +334,24 @@
                 for b in range(2 * SLOTS + INNER, 3 * SLOTS + INNER - 1):
                     gathered[p][k][b] = jnp.zeros((NZ * M, BS), jnp.bfloat16)
 
-    for k in range(CHUNKS):
-        spread_row(0, k)
-    for k in range(CHUNKS):
-        spread_rows(0, k)
-    for p in range(2):
-        for k in range(CHUNKS):
-            exchange(p, k)
-        if p == 0:
-            mask(0)
-            mask(1)
-            sibling_vir().wait_recv()
-        for k in range(CHUNKS):
-            multiply(p, k)
-        for k in range(CHUNKS):
-            finish(p, k)
-            if p == 0:
-                spread_row(1, k)
-        if p == 0:
-            for k in range(CHUNKS):
-                spread_rows(1, k)
+    masked = set()
+    steps = (spread_row, spread_rows, exchange, multiply, finish)
+
+    def do(step, k):
+        if step % 5 == 3 and step not in masked:
+            masked.add(step)
+            mask(step // 5)
+            if step == 3:
+                sibling_vir().wait_recv()
+        steps[step % 5](step // 5, k)
+        if step == 0 and k == CHUNKS - 1:
+            sibling_vir().start()
+            sibling_ints(0).start()
+        if step == 2 and k == CHUNKS - 1:
+            sibling_ints(1).start()
+
+    for step, k in ORDER:
+        do(step, k)
 
     for p in range(2):
         sibling_ints(p).wait_send()
@@ -422,7 +424,17 @@
         occ_energy[:, None],
         vir_energy.reshape(DEVB, 1, BS),
     )
-    return call(True, 1, operands)
+    index = jnp.arange(sym_sizes.shape[0])
+    upto = index[None, :] <= index[:, None]
+    ends = jnp.sum(jnp.where(upto, sym_sizes[None, :], 0), axis=1)
+    starts = ends - sym_sizes
+    inside = (starts // CHIPB == ends // CHIPB) & (starts % CHIPB != 0)
+    return lax.cond(
+        jnp.any(inside),
+        functools.partial(call, True, 1),
+        functools.partial(call, False, 2),
+        operands,
+    )
 
 
 def solution(mesh):

time: 225 us -> 198 us (0.88)
  Pallas kernels: 221 us -> 191 us
    pallas_call x1, Pallas kernels: 221 us -> 191 us  [call(): pl.pallas_call(functools.partial(kernel, inner), name='ladders', out_shap...]
where the time goes in v2:
time: 198 us; the launch traced here: 196 us
  Pallas kernels  191 us (96%)
  local copies, waits for them, and re-layouts  2.45 us (1%)
  other arithmetic  2.08 us (1%)
    pallas_call x1, Pallas kernels, call(): pl.pallas_call(functools.partial(kernel, inner), name='ladders', out_shap...  191 us

profile of v2, /device:TPU:65, one launch (start us, length us, event | category | flops | bytes accessed | tf_op | source)
XLA Modules:
  0.0 196.5 jit_solution(10213020801511138101)
XLA Ops:
  0.0 0.8 select_reduce_fusion
  0.8 1.3 and_reduce_fusion
  2.7 192.8 %conditional.1 = (f32[256,1024]{1,0:T(8,128)S(1)}) conditional(s32[]{:T(128)} %convert_element_type.3, (s32[8]{0:T(128)}, bf16[256,1024]{1,0:T(8,128)(2,1)}, bf16[8,1536,128]{2,1,0:T(8,128)(2,1)}, bf16[8,1536,128]{2,1,0:T(8,128)(2,1)}, f32[256,1]{0,1:T(1,128)}, /*index=5*/f32[8,1,128]{2,1,0:T(1,128)}) %tuple.26, (s32[8]{0:T(128)}, ...), branch_computations={%region_2.3_spmd, %region_3.4_spmd} | conditional | bytes 2056 | solution.py:432
  2.9 1.5 copy.12.occ
  4.4 191.1 %ladders.3 = f32[256,1024]{1,0:T(8,128)S(1)} custom-call(s32[8]{0:T(128)} %get-tuple-element.38.sizes, bf16[256,1024]{1,0:T(8,128)(2,1)} %get-tuple-element.39.amps, bf16[8,1536,128]{2,1,0:T(8,128)(2,1)} %get-tuple-element.40.ints0, bf16[8,1536,128]{2,1,0:T(8,128)(2,1)} %get-tuple-element.41.ints1, f32[256,1]{1,0:T(8,128)} %copy.12.occ, ...), custom_call_target="tpu_custom_call" | custom-call | tf_op jit(solution)/shard_map/cond/branch_1_fun/ladders/pallas_call | solution.py:398
  195.5 1.0 copy.16

commit v3 on v2

--- a/solution.py
+++ b/solution.py
@@ -16,7 +16,7 @@
 CHIPB = 2 * DEVB
 DW = DEVB * BS
 KW = SLOTS * BS
-INNER = 14
+LEVELS = ((0, 0), (5, 1), (12, 1), (14, 2))
 WIN = 7 * CHIPB
 HERE = 3 * CHIPB
 CHUNKS = 8
@@ -42,7 +42,8 @@
     )
 
 
-def kernel(inner, sizes, amps, ints0, ints1, occ, vir, out, *scratch):
+def kernel(level, sizes, amps, ints0, ints1, occ, vir, out, *scratch):
+    (inner, planes) = level
     scratch = list(scratch)
 
     def take(count):
@@ -176,7 +177,7 @@
         return remote(
             packed_in[p][k],
             gathered[p][k].at[
-                pl.ds(2 * SLOTS, INNER), pl.ds(pl.multiple_of(r * M, M), M)
+                pl.ds(2 * SLOTS, inner), pl.ds(pl.multiple_of(r * M, M), M)
             ],
             zi_s.at[p, k, d - 1],
             zi_r.at[p, k, d - 1],
@@ -248,15 +249,15 @@
             z_send(p, k, d).start()
         rows = pl.ds(pl.multiple_of(r * M, M), M)
         if inner:
-            between = source[pl.ds(jnp.clip(inner_at - window_at, 0, WIN - INNER), INNER)]
+            between = source[pl.ds(jnp.clip(inner_at - window_at, 0, WIN - inner), inner)]
             packed_in[p][k][...] = between
             for d in (1, 2, 3):
 
-                @pl.when(z_to(d) < 2)
+                @pl.when(z_to(d) < planes)
                 def _():
                     zi_send(p, k, d).start()
 
-            gathered[p][k][2 * SLOTS : 2 * SLOTS + INNER, rows] = between
+            gathered[p][k][2 * SLOTS : 2 * SLOTS + inner, rows] = between
         gathered[p][k][0:SLOTS, rows] = piece(head, r)
         gathered[p][k][SLOTS : 2 * SLOTS, rows] = piece(tail, r)
 
@@ -265,7 +266,7 @@
             z_send(p, k, d).wait_recv()
         if inner:
 
-            @pl.when(r < 2)
+            @pl.when(r < planes)
             def _():
                 for d in (1, 2, 3):
                     zi_send(p, k, d).wait_recv()
@@ -279,7 +280,7 @@
                 some = count > r * SLOTS
                 place = 2 * SLOTS + first + r * SLOTS - inner_at
                 base = jnp.where(between, jnp.where(some, place, 0), base)
-                base = jnp.clip(base, 0, 2 * SLOTS + INNER - 1)
+                base = jnp.clip(base, 0, 2 * SLOTS + inner - 1)
             tiles = gathered[p][k][pl.ds(base, SLOTS)]
             rows = jnp.concatenate([tiles[i] for i in range(SLOTS)], axis=1)
             product = jnp.dot(rows, ints[p][q], preferred_element_type=jnp.float32)
@@ -331,7 +332,7 @@
     if inner:
         for p in range(2):
             for k in range(CHUNKS):
-                for b in range(2 * SLOTS + INNER, 3 * SLOTS + INNER - 1):
+                for b in range(2 * SLOTS + inner, 3 * SLOTS + inner - 1):
                     gathered[p][k][b] = jnp.zeros((NZ * M, BS), jnp.bfloat16)
 
     masked = set()
@@ -362,7 +363,7 @@
                 p_send(p, k, d).wait_send()
                 if inner:
 
-                    @pl.when(z_to(d) < 2)
+                    @pl.when(z_to(d) < planes)
                     def _():
                         zi_send(p, k, d).wait_send()
 
@@ -374,9 +375,10 @@
         sibling_out(k).wait()
 
 
-def call(inner, number, operands):
+def call(number, operands):
+    inner = LEVELS[number][0]
     bf16, f32 = jnp.bfloat16, jnp.float32
-    width = 2 * SLOTS + (INNER + SLOTS - 1 if inner else 0)
+    width = 2 * SLOTS + (inner + SLOTS - 1 if inner else 0)
     vmem = pltpu.VMEM
     dma = pltpu.SemaphoreType.DMA
     each = []
@@ -384,7 +386,7 @@
     each += [vmem((width, NZ * M, BS), bf16)] * (2 * CHUNKS)
     each += [vmem((3, 2 * SLOTS, M, BS), bf16)] * (2 * CHUNKS)
     if inner:
-        each += [vmem((INNER, M, BS), bf16)] * (2 * CHUNKS)
+        each += [vmem((inner, M, BS), bf16)] * (2 * CHUNKS)
     each += [vmem((CHIPB, KW, BS), bf16)] * 2
     each += [vmem((NZ, CHIPB, M, BS), f32)] * CHUNKS
     each += [vmem((NZ, CHIPB, M, BS), bf16)] * (2 * CHUNKS)
@@ -396,7 +398,7 @@
     each += [dma((2,))] * 3 + [dma((CHUNKS,))] * 2 + [dma(())] * 2 + [dma((CHUNKS,))] * 3
     hbm = pl.BlockSpec(memory_space=pl.ANY)
     return pl.pallas_call(
-        functools.partial(kernel, inner),
+        functools.partial(kernel, LEVELS[number]),
         name="ladders",
         out_shape=jax.ShapeDtypeStruct((2 * ROWS, DW), f32),
         in_specs=[
@@ -410,7 +412,7 @@
         out_specs=hbm,
         scratch_shapes=each,
         compiler_params=pltpu.CompilerParams(
-            collective_id=number, has_side_effects=True, vmem_limit_bytes=60 << 20
+            collective_id=1 + number, has_side_effects=True, vmem_limit_bytes=60 << 20
         ),
     )(*operands)
 
@@ -428,13 +430,13 @@
     upto = index[None, :] <= index[:, None]
     ends = jnp.sum(jnp.where(upto, sym_sizes[None, :], 0), axis=1)
     starts = ends - sym_sizes
-    inside = (starts // CHIPB == ends // CHIPB) & (starts % CHIPB != 0)
-    return lax.cond(
-        jnp.any(inside),
-        functools.partial(call, True, 1),
-        functools.partial(call, False, 2),
-        operands,
-    )
+    chip = starts // CHIPB
+    inside = (chip == ends // CHIPB) & (starts % CHIPB != 0)
+    together = inside[None, :] & (chip[None, :] == chip[:, None])
+    most = jnp.max(jnp.sum(jnp.where(together, sym_sizes[None, :], 0), axis=1))
+    level = sum((most > inner).astype(jnp.int32) for inner, _ in LEVELS[:-1])
+    branches = [functools.partial(call, number) for number in range(len(LEVELS))]
+    return lax.switch(level, branches, operands)
 
 
 def solution(mesh):

time: 198 us -> 194 us (0.980)
  Pallas kernels: 191 us -> 185 us
    pallas_call x1, Pallas kernels: 191 us -> 185 us  [call(): pl.pallas_call(functools.partial(kernel, LEVELS[number]), name='ladders',...]
where the time goes in v3:
time: 194 us
  Pallas kernels  185 us (95%)
  other arithmetic  2.92 us (2%)
  local copies, waits for them, and re-layouts  2.45 us (1%)
  between operations  1.96 us (1%)
    pallas_call x1, Pallas kernels, call(): pl.pallas_call(functools.partial(kernel, LEVELS[number]), name='ladders',...  185 us

profile of v3, /device:TPU:65, one launch (start us, length us, event | category | flops | bytes accessed | tf_op | source)
XLA Modules:
  0.0 193.6 jit_solution(17386623964000218482)
XLA Ops:
  0.0 0.8 select_reduce_fusion.1
  0.8 0.7 compare_and_fusion
  1.4 0.8 select_reduce_fusion
  2.3 0.6 reduce_max.9
  4.9 187.7 %conditional.1 = (f32[256,1024]{1,0:T(8,128)S(1)}) conditional(s32[]{:T(128)} %clamp.3, (s32[8]{0:T(128)}, bf16[256,1024]{1,0:T(8,128)(2,1)}, bf16[8,1536,128]{2,1,0:T(8,128)(2,1)}, bf16[8,1536,128]{2,1,0:T(8,128)(2,1)}, f32[256,1]{0,1:T(1,128)}, /*index=5*/f32[8,1,128]{2,1,0:T(1,128)}) %tuple.47, (s32[8]{0:T(128)}, ...), branch_computations={%region_3.4_spmd, %region_4.5_spmd, %region_5.6_spmd, %region_6.7_... | conditional | bytes 2056 | solution.py:439
  5.1 1.5 copy.17.occ
  6.6 185.4 %ladders.6 = f32[256,1024]{1,0:T(8,128)S(1)} custom-call(s32[8]{0:T(128)} %get-tuple-element.70.sizes, bf16[256,1024]{1,0:T(8,128)(2,1)} %get-tuple-element.71.amps, bf16[8,1536,128]{2,1,0:T(8,128)(2,1)} %get-tuple-element.72.ints0, bf16[8,1536,128]{2,1,0:T(8,128)(2,1)} %get-tuple-element.73.ints1, f32[256,1]{1,0:T(8,128)} %copy.17.occ, ...), custom_call_target="tpu_custom_call" | custom-call | tf_op jit(solution)/shard_map/cond/branch_2_fun/ladders/pallas_call | solution.py:400
  192.6 1.0 copy.24
